TPU v7x, 256 devices: a whole 4x4x8 slice. The times are simulated.
256 devices in a mesh: dom: 32 (over z, x), grp: 8 (over y, core).
Axes of the slice: x: 4, y: 4, z: 8, core: 2. Of those that a mesh axis runs over, the one named last changes fastest.
Arguments:
- heads: int32 [2097152], P(('dom', 'grp')), may hold values from 0 to 4095
- tails: int32 [2097152], P(('dom', 'grp')), may hold values from 0 to 8191, as said below
- signs: int32 [2, 2097152], P(None, ('dom', 'grp')), may hold values from 0 to 4095
- edge_weights: float32 [2097152], P(('dom', 'grp')), may hold values from 0.25 to 4
- ground: float32 [131072], P(('dom', 'grp')), may hold values from 2 to 40
Outputs:
- solution: float32 [24, 131072], P(None, ('dom', 'grp'))
- residual: float32 [24, 131072], P(None, ('dom', 'grp'))
Inputs may be any that keep to these rules, and one draw needn't show every extreme that they name: `tails`: every second endpoint is a vertex of the graph.
All inputs are finite; a program needn't handle non-finite values.
Results may differ from a plain program's by a relative error of at most 0.0003.
Values sent between devices are 32-bit elements; how exact they have to be, the bound alone decides.
A program may use at most 64 MiB of HBM per device.

v0:
```python
import jax
import jax.numpy as jnp
from jax import lax
from jax.sharding import PartitionSpec as P

K = 24
ITERS = 3


def passed_along(value, axis, steps):
    count = lax.axis_size(axis)
    leading, last = (max(0, -steps), min(count, count - steps))
    return lax.ppermute(value, axis, [(source, source + steps) for source in range(leading, last)])


def extended(cells, sides, width):
    for axis, dim in sides:
        count = lax.axis_size(axis)
        ends = count - 1
        head = lax.slice_in_dim(cells, 0, width, axis=dim)
        tail = lax.slice_in_dim(cells, cells.shape[dim] - width, cells.shape[dim], axis=dim)
        cells = jnp.concatenate(
            [
                lax.ppermute(tail, axis, [(i, (i + 1) % count) for i in range(ends)]),
                cells,
                lax.ppermute(head, axis, [((i + 1) % count, i) for i in range(ends)]),
            ],
            axis=dim,
        )
    return cells


def unpack(signs):
    half = K // 2
    shifts = jnp.arange(half, dtype=jnp.int32)
    bits = jnp.right_shift(signs[:, None, :], shifts[None, :, None]) & 1
    return (2 * bits - 1).reshape(2 * half, -1).astype(jnp.float32)


def on_device(heads, tails, signs, edge_weights, ground):
    verts = ground.shape[0]
    domain = verts * lax.axis_size("grp")
    reach = domain // 2
    extent = domain + 2 * reach
    first = heads + reach

    def edge_scatter(plus, minus):
        acc = jnp.zeros((plus.shape[0], extent), jnp.float32)
        return acc.at[:, first].add(plus).at[:, tails].add(minus)

    def fold(acc):
        middle = acc[:, reach : reach + domain]
        received = []
        for offset in (1, -1):
            border = acc[:, reach + domain :] if offset == 1 else acc[:, :reach]
            received.append(passed_along(border, "dom", offset))
        middle = middle + jnp.concatenate(received, axis=1)
        return lax.psum_scatter(middle, "grp", scatter_dimension=1, tiled=True)

    def inner(pairs):
        partial_value = tuple((jnp.sum(left * right_term, axis=1) for left, right_term in pairs))
        return lax.psum(partial_value, ("dom", "grp"))

    scaled = unpack(signs) * jnp.sqrt(edge_weights)[None, :]
    plus = jnp.concatenate([scaled, edge_weights[None, :]], axis=0)
    minus = jnp.concatenate([-scaled, edge_weights[None, :]], axis=0)
    gathered = fold(edge_scatter(plus, minus))
    right = gathered[:K]
    diag = gathered[K] + ground
    solution = jnp.zeros_like(right)
    residual = right
    scaled_res = residual / diag[None, :]
    direction = scaled_res
    (gamma,) = inner(((residual, scaled_res),))
    for step in range(ITERS):
        whole = lax.all_gather(direction, "grp", axis=1, tiled=True)
        widened = extended(whole, (("dom", 1),), reach)
        diff = edge_weights[None, :] * (widened[:, first] - widened[:, tails])
        image = fold(edge_scatter(diff, -diff)) + ground[None, :] * direction
        (curvature,) = inner(((direction, image),))
        alpha = gamma / curvature
        solution = solution + alpha[:, None] * direction
        residual = residual - alpha[:, None] * image
        scaled_res = residual / diag[None, :]
        (following,) = inner(((residual, scaled_res),))
        direction = scaled_res + (following / gamma)[:, None] * direction
        gamma = following
    return (solution, residual)


def solution(mesh):
    in_specs = (
        P(("dom", "grp")),
        P(("dom", "grp")),
        P(None, ("dom", "grp")),
        P(("dom", "grp")),
        P(("dom", "grp")),
    )
    out_specs = (P(None, ("dom", "grp")), P(None, ("dom", "grp")))
    return jax.shard_map(
        on_device, mesh=mesh, in_specs=in_specs, out_specs=out_specs, check_vma=False
    )
```

profile of v0, /device:TPU:1, one launch (start us, length us, event | category | flops | bytes accessed | tf_op | source)
XLA Modules:
  0.0 1285.3 jit_solution(4227813058469706701)
XLA Ops:
  16.5 46.5 %scatter_custom_fusion = f32[25,8192]{0,1:T(8,128)} fusion(s32[8192]{0:T(1024)S(1)} %get-tuple-element.39, f32[8192,25]{1,0:T(8,128)} %copy.73, f32[]{:T(128)} %constant.2.clone.1), kind=kCustom, calls=%fused_computation.29 | custom fusion | flops 204800 | bytes 819712 | tf_op jit(solution)/shard_map/scatter-add | solution.py:49
  63.0 44.0 %scatter_fusion = f32[25,8192]{0,1:T(8,128)} fusion(f32[25,8192]{0,1:T(8,128)} %scatter_custom_fusion, s32[8192]{0:T(1024)S(1)} %get-tuple-element.37, f32[8192,25]{1,0:T(8,128)} %copy.74), kind=kCustom, calls=%fused_computation.7 | custom fusion | flops 204800 | bytes 2490368 | tf_op jit(solution)/shard_map/scatter-add | solution.py:49
  110.6 5.4 collective-permute-start
  120.5 40.7 %reduce-scatter.5.cloned.1.call-done = f32[25,512]{1,0:T(8,128)} async-done(((f32[25,4096]{1,0:T(8,128)}), f32[25,512]{1,0:T(8,128)}) %reduce-scatter.5.cloned.1.call-update) | async-done | bytes 51216 | tf_op jit(solution)/shard_map/reduce_scatter | solution.py:58
  162.8 15.9 %all_gather.9 = f32[24,4096]{1,0:T(8,128)S(1)} all-gather(f32[24,512]{1,0:T(8,128)S(1)} %slice_divide_fusion), channel_id=1, replica_groups=mesh['dom'=32,'grp'=8] {'grp'}, dimensions={1}, use_global_device_ids=true | all-gather | bytes 442368 | tf_op jit(solution)/shard_map/all_gather | solution.py:76
  185.9 3.8 collective-permute-done.3
  192.4 29.9 %gather_fusion.1 = f32[8192,24]{1,0:T(8,128)} fusion(f32[24,8192]{0,1:T(8,128)} %copy.78, s32[8192]{0:T(1024)S(1)} %get-tuple-element.36), kind=kCustom, calls=%fused_computation.1 | custom fusion | bytes 1605632 | tf_op jit(solution)/shard_map/gather | solution.py:78
  222.3 29.9 %gather_fusion = f32[8192,24]{1,0:T(8,128)} fusion(f32[24,8192]{0,1:T(8,128)} %copy.78, s32[8192]{0:T(1024)S(1)} %get-tuple-element.38), kind=kCustom, calls=%fused_computation | custom fusion | bytes 1605632 | tf_op jit(solution)/shard_map/gather | solution.py:78
  252.2 50.8 %scatter_custom_fusion.2 = f32[24,8192]{0,1:T(8,128)} fusion(s32[8192]{0:T(1024)} %copy-done.4, f32[]{:T(128)} %constant.2.clone.1, f32[8192,24]{1,0:T(8,128)} %gather_fusion, f32[8192,24]{1,0:T(8,128)} %gather_fusion.1, f32[8192]{0:T(1024)S(1)} %copy-done), kind=kCustom, calls=%fused_computation.27 | custom fusion | flops 589824 | bytes 9208320 | tf_op jit(solution)/shard_map/scatter-add | solution.py:49
  303.0 52.7 %scatter_custom_fusion.3 = f32[24,8192]{0,1:T(8,128)} fusion(f32[24,8192]{0,1:T(8,128)} %scatter_custom_fusion.2, s32[8192]{0:T(1024)S(1)} %get-tuple-element.37, f32[8192,24]{1,0:T(8,128)} %gather_fusion, f32[8192,24]{1,0:T(8,128)} %gather_fusion.1, f32[8192]{0:T(1024)S(1)} %copy-done), kind=kCustom, calls=%fused_computation.18 | custom fusion | flops 786432 | bytes 9207808 | tf_op jit(solution)/shard_map/scatter-add | solution.py:49
  359.5 4.0 collective-permute-start.4
  366.9 41.0 %reduce-scatter.7.cloned.1.call-done = f32[24,512]{1,0:T(8,128)} async-done(((f32[24,4096]{1,0:T(8,128)}), f32[24,512]{1,0:T(8,128)}) %reduce-scatter.7.cloned.1.call-update) | async-done | bytes 49168 | tf_op jit(solution)/shard_map/reduce_scatter | solution.py:58
  408.9 78.4 %all-reduce = (f32[24]{0:T(128)S(1)}, f32[24]{0:T(128)S(1)}) all-reduce(f32[24]{0:T(128)S(1)} %get-tuple-element.11, f32[24]{0:T(128)S(1)} %get-tuple-element.10), channel_id=1, replica_groups=mesh['dom'=32,'grp'=8] {'dom','grp'}, use_global_device_ids=true, to_apply=%region_4.0 | all-reduce | flops 48 | bytes 384 | tf_op jit(solution)/shard_map/psum | solution.py:62
  488.3 73.2 %psum.44 = f32[24]{0:T(128)S(1)} all-reduce(f32[24]{0:T(128)S(1)} %get-tuple-element.16), channel_id=1, replica_groups=mesh['dom'=32,'grp'=8] {'dom','grp'}, use_global_device_ids=true, to_apply=%region_11.0 | all-reduce | flops 24 | bytes 192 | tf_op jit(solution)/shard_map/psum | solution.py:62
  561.6 13.5 %all_gather.10 = f32[24,4096]{1,0:T(8,128)S(1)} all-gather(f32[24,512]{1,0:T(8,128)S(1)} %multiply_add_fusion.4), channel_id=1, replica_groups=mesh['dom'=32,'grp'=8] {'grp'}, dimensions={1}, use_global_device_ids=true | all-gather | bytes 442368 | tf_op jit(solution)/shard_map/all_gather | solution.py:76
  588.0 29.9 %gather_fusion.3 = f32[8192,24]{1,0:T(8,128)} fusion(f32[24,8192]{0,1:T(8,128)} %copy.83, s32[8192]{0:T(1024)S(1)} %get-tuple-element.36), kind=kCustom, calls=%fused_computation.3 | custom fusion | bytes 1605632 | tf_op jit(solution)/shard_map/gather | solution.py:78
  617.9 29.9 %gather_fusion.2 = f32[8192,24]{1,0:T(8,128)} fusion(f32[24,8192]{0,1:T(8,128)} %copy.83, s32[8192]{0:T(1024)S(1)} %get-tuple-element.38), kind=kCustom, calls=%fused_computation.2 | custom fusion | bytes 1605632 | tf_op jit(solution)/shard_map/gather | solution.py:78
  647.8 50.8 %scatter_custom_fusion.4 = f32[24,8192]{0,1:T(8,128)} fusion(s32[8192]{0:T(1024)} %copy-done.4, f32[]{:T(128)} %constant.2.clone.1, f32[8192,24]{1,0:T(8,128)} %gather_fusion.2, f32[8192,24]{1,0:T(8,128)} %gather_fusion.3, f32[8192]{0:T(1024)S(1)} %copy-done), kind=kCustom, calls=%fused_computation.25 | custom fusion | flops 589824 | bytes 9208320 | tf_op jit(solution)/shard_map/scatter-add | solution.py:49
  698.6 52.7 %scatter_custom_fusion.5 = f32[24,8192]{0,1:T(8,128)} fusion(f32[24,8192]{0,1:T(8,128)} %scatter_custom_fusion.4, s32[8192]{0:T(1024)} %copy-done.2, f32[8192,24]{1,0:T(8,128)} %gather_fusion.2, f32[8192,24]{1,0:T(8,128)} %gather_fusion.3, f32[8192]{0:T(1024)S(1)} %copy-done), kind=kCustom, calls=%fused_computation.16 | custom fusion | flops 786432 | bytes 9207808 | tf_op jit(solution)/shard_map/scatter-add | solution.py:49
  754.9 4.0 collective-permute-start.8
  762.4 40.2 %reduce-scatter.9.cloned.1.call-done = f32[24,512]{1,0:T(8,128)} async-done(((f32[24,4096]{1,0:T(8,128)}), f32[24,512]{1,0:T(8,128)}) %reduce-scatter.9.cloned.1.call-update) | async-done | bytes 49168 | tf_op jit(solution)/shard_map/reduce_scatter | solution.py:58
  803.5 78.4 %psum.45 = f32[24]{0:T(128)S(1)} all-reduce(f32[24]{0:T(128)S(1)} %multiply_reduce_fusion.2), channel_id=1, replica_groups=mesh['dom'=32,'grp'=8] {'dom','grp'}, use_global_device_ids=true, to_apply=%region_16.0 | all-reduce | flops 24 | bytes 192 | tf_op jit(solution)/shard_map/psum | solution.py:62
  882.9 73.2 %psum.46 = f32[24]{0:T(128)S(1)} all-reduce(f32[24]{0:T(128)S(1)} %get-tuple-element.14), channel_id=1, replica_groups=mesh['dom'=32,'grp'=8] {'dom','grp'}, use_global_device_ids=true, to_apply=%region_18.0 | all-reduce | flops 24 | bytes 192 | tf_op jit(solution)/shard_map/psum | solution.py:62
  956.2 13.5 %all_gather.11 = f32[24,4096]{1,0:T(8,128)S(1)} all-gather(f32[24,512]{1,0:T(8,128)S(1)} %multiply_add_fusion.2), channel_id=1, replica_groups=mesh['dom'=32,'grp'=8] {'grp'}, dimensions={1}, use_global_device_ids=true | all-gather | bytes 442368 | tf_op jit(solution)/shard_map/all_gather | solution.py:76
  976.2 3.8 collective-permute-done.11
  982.7 29.9 %gather_fusion.5 = f32[8192,24]{1,0:T(8,128)} fusion(f32[24,8192]{0,1:T(8,128)} %copy.88, s32[8192]{0:T(1024)S(1)} %get-tuple-element.36), kind=kCustom, calls=%fused_computation.5 | custom fusion | bytes 1605632 | tf_op jit(solution)/shard_map/gather | solution.py:78
  1012.6 29.9 %gather_fusion.4 = f32[8192,24]{1,0:T(8,128)} fusion(f32[24,8192]{0,1:T(8,128)} %copy.88, s32[8192]{0:T(1024)S(1)} %get-tuple-element.38), kind=kCustom, calls=%fused_computation.4 | custom fusion | bytes 1605632 | tf_op jit(solution)/shard_map/gather | solution.py:78
  1042.5 50.8 %scatter_custom_fusion.6 = f32[24,8192]{0,1:T(8,128)} fusion(s32[8192]{0:T(1024)} %copy-done.4, f32[]{:T(128)} %constant.2.clone.1, f32[8192,24]{1,0:T(8,128)} %gather_fusion.4, f32[8192,24]{1,0:T(8,128)} %gather_fusion.5, f32[8192]{0:T(1024)S(1)} %copy-done), kind=kCustom, calls=%fused_computation.23 | custom fusion | flops 589824 | bytes 9208320 | tf_op jit(solution)/shard_map/scatter-add | solution.py:49
  1093.3 52.7 %scatter_custom_fusion.7 = f32[24,8192]{0,1:T(8,128)} fusion(f32[24,8192]{0,1:T(8,128)} %scatter_custom_fusion.6, s32[8192]{0:T(1024)} %copy-done.2, f32[8192,24]{1,0:T(8,128)} %gather_fusion.4, f32[8192,24]{1,0:T(8,128)} %gather_fusion.5, f32[8192]{0:T(1024)S(1)} %copy-done), kind=kCustom, calls=%fused_computation.14 | custom fusion | flops 786432 | bytes 9207808 | tf_op jit(solution)/shard_map/scatter-add | solution.py:49
  1150.3 4.0 collective-permute-start.12
  1157.7 40.3 %reduce-scatter.11.cloned.1.call-done = f32[24,512]{1,0:T(8,128)} async-done(((f32[24,4096]{1,0:T(8,128)}), f32[24,512]{1,0:T(8,128)}) %reduce-scatter.11.cloned.1.call-update) | async-done | bytes 49168 | tf_op jit(solution)/shard_map/reduce_scatter | solution.py:58
  1198.9 78.4 %psum.47 = f32[24]{0:T(128)S(1)} all-reduce(f32[24]{0:T(128)S(1)} %multiply_reduce_fusion), channel_id=1, replica_groups=mesh['dom'=32,'grp'=8] {'dom','grp'}, use_global_device_ids=true, to_apply=%region_23.0 | all-reduce | flops 24 | bytes 192 | tf_op jit(solution)/shard_map/psum | solution.py:62
  (100 shorter events, 79.1 us)
Async XLA Ops:
  7.2 3.8 copy-start
  7.2 154.1 %reduce-scatter.5.cloned.1.call-start = ((), (), s32[]{:S(2)}) async-start(), calls=%async_computation.4 | async-start | bytes 589824 | tf_op jit(solution)/shard_map/reduce_scatter | solution.py:58
  8.9 7.6 copy-start.4
  9.7 293.4 %copy-start.2 = (s32[8192]{0:T(1024)}, s32[8192]{0:T(1024)S(1)}, u32[]{:S(2)}) copy-start(s32[8192]{0:T(1024)S(1)} %get-tuple-element.37) | copy-start | bytes 98308
  109.0 9.4 collective-permute-start.1
  110.6 51.3 %copy-start.3 = (f32[512]{0:T(512)S(1)}, f32[512]{0:T(512)}, u32[]{:S(2)}) copy-start(f32[512]{0:T(512)} %param.9) | copy-start | bytes 6148
  110.6 8.0 collective-permute-start
  120.5 287.5 %reduce-scatter.7.cloned.1.call-start = ((), (), s32[]{:S(2)}) async-start(), calls=%async_computation.5 | async-start | bytes 442368 | tf_op jit(solution)/shard_map/reduce_scatter | solution.py:58
  178.7 7.2 collective-permute-start.2
  181.8 7.9 collective-permute-start.3
  358.0 49.9 %copy-start.1 = (f32[25,512]{1,0:T(8,128)S(1)}, f32[25,512]{1,0:T(8,128)}, u32[]{:S(2)}) copy-start(f32[25,512]{1,0:T(8,128)} %reduce-scatter.5.cloned.1.call-done) | copy-start | bytes 153604
  358.0 7.7 collective-permute-start.5
  359.5 6.6 collective-permute-start.4
  366.9 435.7 %reduce-scatter.9.cloned.1.call-start = ((), (), s32[]{:S(2)}) async-start(), calls=%async_computation.6 | async-start | bytes 442368 | tf_op jit(solution)/shard_map/reduce_scatter | solution.py:58
  575.1 6.4 collective-permute-start.6
  577.4 7.9 collective-permute-start.7
  753.6 7.6 collective-permute-start.9
  754.9 6.6 collective-permute-start.8
  762.3 435.6 %reduce-scatter.11.cloned.1.call-start = ((), (), s32[]{:S(2)}) async-start(), calls=%async_computation.7 | async-start | bytes 442368 | tf_op jit(solution)/shard_map/reduce_scatter | solution.py:58
  969.7 6.4 collective-permute-start.10
  972.0 7.9 collective-permute-start.11
  1149.0 7.6 collective-permute-start.13
  1150.3 6.6 collective-permute-start.12
Sparse Core Ops, SparseCore 0:
  120.6 40.6 reduce-scatter.4
  367.0 40.9 reduce-scatter.6
  762.4 40.1 reduce-scatter.8
  1157.8 40.1 reduce-scatter.10
where the time goes:
time: 1290 us
  blocking collectives  424 us (33%)
  other arithmetic  415 us (32%)
  local copies, waits for them, and re-layouts  215 us (17%)
  waiting for transfers between devices  183 us (14%)
  starting transfers between devices  34.4 us (3%)
  between operations  14 us (1%)
    scatter-add x8, other arithmetic, edge_scatter(): return acc.at[:, first].add(plus).at[:, tails].add(minus)  401 us
    psum x5, blocking collectives, inner(): return lax.psum(partial_value, ('dom', 'grp'))  382 us
    gather x6, local copies, waits for them, and re-layouts, on_device(): diff = edge_weights[None, :] * (widened[:, first] - widened[:, tails])  179 us
    reduce_scatter x4, waiting for transfers between devices, fold(): return lax.psum_scatter(middle, 'grp', scatter_dimension=1, tiled=True)  162 us
    all_gather x3, blocking collectives, on_device(): whole = lax.all_gather(direction, 'grp', axis=1, tiled=True)  42.8 us
  transfers between devices with their start and end apart: 18, of which 14 were waited for; matrix products, arithmetic and copies ran while one was open for 1% of the time, Pallas kernels for 0%

commit v1 on v0

v1 whole, which is shorter than its diff:
```python
import functools

import jax
import jax.numpy as jnp
from jax import lax
from jax.experimental import pallas as pl
from jax.experimental.pallas import tpu as pltpu
from jax.sharding import PartitionSpec as P

MESH = pl.DeviceIdType.MESH
BF, F, I = jnp.bfloat16, jnp.float32, jnp.int32
NT = (((1,), (1,)), ((), ()))
K = 24
ITERS = 3
NX, NZ, NY = 4, 8, 4
OWN = 3
ROWS = 2 * OWN
LANES = 256
WIN, MID, SIDE = 32, 16, 8
EC = 4096


def split(value):
    high = value.astype(BF)
    return high, (value - high.astype(F)).astype(BF)


def onehot(index):
    lanes = lax.broadcasted_iota(I, (LANES, index.shape[1]), 0).astype(F).astype(BF)
    return jnp.where(lanes == index.astype(F).astype(BF), jnp.ones((), BF), jnp.zeros((), BF))


def edge_rows(eb, c):
    block, row = c // 2, c % 2
    heads = eb[block, pl.ds(row, 1), :].astype(I)
    tails = eb[block, pl.ds(2 + row, 1), :].astype(I)
    weight = eb[block, pl.ds(4 + row, 1), :]
    return block, row, heads, tails, weight


def masks(heads, tails):
    ec = heads.shape[1]
    at_tail = lax.broadcasted_iota(I, (WIN, ec), 0) == (tails >> 8)
    at_head = lax.broadcasted_iota(I, (MID, ec), 0) == (heads >> 8)
    return at_tail, at_head


def spread(mask, parts):
    ones = jnp.where(mask, 1.0, 0.0).astype(BF)
    return jnp.concatenate([ones * parts[k][q] for q in range(2) for k in range(len(parts))], axis=0)


def sketch_edges(eb, shift, total_t, total_h, acc):
    rows = ROWS + 1
    nt, nh = rows * WIN, rows * MID
    total_t[...] = jnp.zeros_like(total_t)
    total_h[...] = jnp.zeros_like(total_h)

    def body(c, carry):
        block, row, heads, tails, weight = edge_rows(eb, c)
        bits = eb[block, pl.ds(6 + row, 1), :].astype(I) >> shift
        at_tail, at_head = masks(heads, tails)
        root = jnp.sqrt(weight)
        high, low = split(root)
        high, low = high.astype(F), low.astype(F)
        parts = []
        for k in range(ROWS):
            positive = ((bits >> k) & 1) == 1
            parts.append(
                (jnp.where(positive, high, -high).astype(BF), jnp.where(positive, low, -low).astype(BF))
            )
        w_high, w_low = split(weight)
        total_t[...] += lax.dot_general(
            spread(at_tail, parts + [(-w_high, -w_low)]), onehot(tails & 255), NT, preferred_element_type=F
        )
        total_h[...] += lax.dot_general(
            spread(at_head, parts + [(w_high, w_low)]), onehot(heads & 255), NT, preferred_element_type=F
        )
        return carry

    lax.fori_loop(0, 2 * NY, body, 0)
    both = -(total_t[:nt] + total_t[nt:]).reshape(rows, WIN, LANES)
    middle = (total_h[:nh] + total_h[nh:]).reshape(rows, MID, LANES)
    for core in range(2):
        for k in range(OWN + 1):
            source = OWN * core + k if k < OWN else ROWS
            acc[core, k] = both[source]
            acc[core, k, SIDE : SIDE + MID] += middle[source]


def apply_edges(eb, table, tab_t, tab_h, total_t, total_h, acc):
    nt, nh = ROWS * WIN, ROWS * MID
    for core in range(2):
        high, low = split(table[core])
        at, ah = OWN * core * WIN, OWN * core * MID
        tab_t[at : at + OWN * WIN] = high.reshape(OWN * WIN, LANES)
        tab_t[nt + at : nt + at + OWN * WIN] = low.reshape(OWN * WIN, LANES)
        tab_h[ah : ah + OWN * MID] = high[:, SIDE : SIDE + MID].reshape(OWN * MID, LANES)
        tab_h[nh + ah : nh + ah + OWN * MID] = low[:, SIDE : SIDE + MID].reshape(OWN * MID, LANES)
    total_t[...] = jnp.zeros_like(total_t)
    total_h[...] = jnp.zeros_like(total_h)

    def body(c, carry):
        _, _, heads, tails, weight = edge_rows(eb, c)
        at_tail, at_head = masks(heads, tails)
        hot_t, hot_h = onehot(tails & 255), onehot(heads & 255)
        from_t = jnp.dot(tab_t[...], hot_t, preferred_element_type=F)
        from_h = jnp.dot(tab_h[...], hot_h, preferred_element_type=F)
        parts = []
        for k in range(ROWS):
            t_rows = from_t[WIN * k : WIN * (k + 1)] + from_t[nt + WIN * k : nt + WIN * (k + 1)]
            h_rows = from_h[MID * k : MID * (k + 1)] + from_h[nh + MID * k : nh + MID * (k + 1)]
            t_sum = jnp.where(at_tail, t_rows, 0.0).reshape(WIN // 8, 8, EC).sum(0)
            h_sum = jnp.where(at_head, h_rows, 0.0).reshape(MID // 8, 8, EC).sum(0)
            parts.append(split(weight * jnp.sum(h_sum - t_sum, axis=0, keepdims=True)))
        total_t[: 2 * nt] += lax.dot_general(spread(at_tail, parts), hot_t, NT, preferred_element_type=F)
        total_h[: 2 * nh] += lax.dot_general(spread(at_head, parts), hot_h, NT, preferred_element_type=F)
        return carry

    lax.fori_loop(0, 2 * NY, body, 0)
    both = -(total_t[:nt] + total_t[nt : 2 * nt]).reshape(ROWS, WIN, LANES)
    middle = (total_h[:nh] + total_h[nh : 2 * nh]).reshape(ROWS, MID, LANES)
    for core in range(2):
        for k in range(OWN):
            acc[core, k] = both[OWN * core + k]
            acc[core, k, SIDE : SIDE + MID] += middle[OWN * core + k]


def kernel(
    edges, ground, sol, res,
    eb, gb, table, acc, in_mid, in_left, in_right,
    tab_t, tab_h, total_t, total_h, state, stat_x, stat_z, out_s, out_r,
    ag_s, ag_r, gr_s, gr_r, a_s, a_r, b_s, b_r, x_s, x_r, z_s, z_r, o_s, o_r,
):
    dom, grp = lax.axis_index("dom"), lax.axis_index("grp")
    z, x = dom // NX, dom % NX
    y, core = grp // 2, grp % 2
    other = 1 - core
    left, right = (dom + NX * NZ - 1) % (NX * NZ), (dom + 1) % (NX * NZ)
    near = [(dom, 2 * y + other)]
    near += [(left, 2 * y + (core + rc) % 2) for rc in range(2)]
    near += [(right, 2 * y + (core + rc) % 2) for rc in range(2)]
    group = [(dom, (grp + j) % 8) for j in range(1, 8)]
    along_x = [(z * NX + (x + j) % NX, grp) for j in range(1, NX)]
    along_z = [(((z + j) % NZ) * NX + x, grp) for j in range(1, NZ)]

    stat_x[...] = jnp.zeros_like(stat_x)
    barrier = pltpu.get_barrier_semaphore()
    peers = group + near[1:] + along_x + along_z
    for peer in peers:
        pl.semaphore_signal(barrier, inc=1, device_id=peer, device_id_type=MESH)
    pl.semaphore_wait(barrier, len(peers))

    def send(source, target, sems, at, peer):
        copy = pltpu.make_async_remote_copy(
            src_ref=source, dst_ref=target, send_sem=sems[0].at[at], recv_sem=sems[1].at[at],
            device_id=peer, device_id_type=MESH,
        )
        copy.start()
        return copy

    def finish(copies):
        for copy in copies:
            copy.wait()

    copies = []
    for j in range(1, NY):
        to = (y + j) % NY
        copies.append(send(edges.at[to // 2], eb.at[y], (ag_s, ag_r), j - 1, (dom, 2 * to + core)))
    for j in range(1, 8):
        copies.append(send(ground, gb.at[grp], (gr_s, gr_r), j - 1, group[j - 1]))
    eb[y] = edges[y // 2]
    gb[grp] = ground[...]
    finish(copies)

    def fold(rows):
        sems = (b_s, b_r)
        copies = [send(acc.at[other, :rows, SIDE : SIDE + MID], in_mid.at[:rows], sems, 0, near[0])]
        for rc in range(2):
            theirs = (core + rc) % 2
            copies.append(send(acc.at[theirs, :rows, :SIDE], in_right.at[rc, :rows], sems, 1 + rc, near[1 + rc]))
            copies.append(
                send(acc.at[theirs, :rows, SIDE + MID :], in_left.at[rc, :rows], sems, 3 + rc, near[3 + rc])
            )
        finish(copies)
        sums = []
        for k in range(rows):
            low = in_left[0, k] + in_left[1, k]
            high = in_right[0, k] + in_right[1, k]
            sums.append(acc[core, k, SIDE : SIDE + MID] + in_mid[k] + jnp.concatenate([low, high], axis=0))
        return sums

    def share():
        sems = (a_s, a_r)
        mine = table.at[core]
        copies = [send(mine.at[:, SIDE : SIDE + MID], mine.at[:, SIDE : SIDE + MID], sems, 0, near[0])]
        for rc in range(2):
            copies.append(send(mine.at[:, SIDE : 2 * SIDE], mine.at[:, SIDE + MID :], sems, 1 + rc, near[1 + rc]))
            copies.append(send(mine.at[:, MID : SIDE + MID], mine.at[:, :SIDE], sems, 3 + rc, near[3 + rc]))
        finish(copies)

    def reduce_all(it, values):
        for row, value in enumerate(values):
            lanes = jnp.sum(value, axis=0, keepdims=True)
            stat_x[it, x, row : row + 1, :] = lanes[:, :128] + lanes[:, 128:]
        copies = []
        for j in range(1, NX):
            here = stat_x.at[it, x]
            copies.append(send(here, here, (x_s.at[it], x_r.at[it]), j - 1, along_x[j - 1]))
        finish(copies)
        stat_z[it, z] = (stat_x[it, 0] + stat_x[it, 1]) + (stat_x[it, 2] + stat_x[it, 3])
        copies = []
        for j in range(1, NZ):
            here = stat_z.at[it, z]
            copies.append(send(here, here, (z_s.at[it], z_r.at[it]), j - 1, along_z[j - 1]))
        finish(copies)
        whole = stat_z[it, 0]
        for j in range(1, NZ):
            whole = whole + stat_z[it, j]
        return jnp.sum(whole, axis=1, keepdims=True)

    DIAG, GROUND, R, PP, S, X = 0, 1, 2, 2 + OWN, 2 + 2 * OWN, 2 + 3 * OWN
    for j in range(8):
        state[GROUND, 2 * j : 2 * j + 2, :] = gb[j]
    sketch_edges(eb, 6 * (y % 2), total_t, total_h, acc)
    sums = fold(OWN + 1)
    state[DIAG] = sums[OWN] + state[GROUND]
    for k in range(OWN):
        state[R + k] = sums[k]
        table[core, k, SIDE : SIDE + MID] = sums[k] / state[DIAG]

    gamma_was = curve_was = None
    for it in range(ITERS):
        share()
        apply_edges(eb, table, tab_t, tab_h, total_t, total_h, acc)
        sums = fold(OWN)
        u = [table[core, k, SIDE : SIDE + MID] for k in range(OWN)]
        image = [sums[k] + state[GROUND] * u[k] for k in range(OWN)]
        values = [state[R + k] * u[k] for k in range(OWN)] + [u[k] * image[k] for k in range(OWN)]
        if it:
            values += [u[k] * state[S + k] for k in range(OWN)]
        totals = reduce_all(it, values)
        gamma, curve = totals[:OWN], totals[OWN : 2 * OWN]
        if it:
            beta = gamma / gamma_was
            curve = curve + 2.0 * beta * totals[2 * OWN : 3 * OWN] + beta * beta * curve_was
        alpha = gamma / curve
        for k in range(OWN):
            a = alpha[k : k + 1]
            if it:
                b = beta[k : k + 1]
                direction = u[k] + b * state[PP + k]
                along = image[k] + b * state[S + k]
                state[X + k] = state[X + k] + a * direction
            else:
                direction, along = u[k], image[k]
                state[X + k] = a * direction
            state[PP + k] = direction
            state[S + k] = along
            rest = state[R + k] - a * along
            state[R + k] = rest
            if it < ITERS - 1:
                table[core, k, SIDE : SIDE + MID] = rest / state[DIAG]
        gamma_was, curve_was = gamma, curve

    for g in range(8):
        for k in range(OWN):
            for half in range(2):
                lanes = slice(LANES * half, LANES * (half + 1))
                tile = slice(2 * g + half, 2 * g + half + 1)
                out_s[g, k : k + 1, lanes] = state[X + k, tile, :]
                out_s[g, OWN + k : OWN + k + 1, lanes] = state[R + k, tile, :]
    copies = []
    for j in range(1, 8):
        to = (grp + j) % 8
        copies.append(send(out_s.at[to], out_r.at[grp], (o_s, o_r), j - 1, group[j - 1]))
    out_r[grp] = out_s[grp]
    finish(copies)
    for g in range(8):
        sol[OWN * g : OWN * (g + 1), :] = out_r[g, :OWN, :]
        res[OWN * g : OWN * (g + 1), :] = out_r[g, OWN : 2 * OWN, :]


def on_device(heads, tails, signs, edge_weights, ground):
    common = [heads.astype(F).reshape(2, EC), tails.astype(F).reshape(2, EC), edge_weights.reshape(2, EC)]
    words = signs.astype(F).reshape(2, 2, EC)
    edges = jnp.stack([jnp.concatenate(common + [words[j]], axis=0) for j in range(2)])
    dma = lambda *shape: pltpu.SemaphoreType.DMA(shape)
    vmem = pl.BlockSpec(memory_space=pltpu.VMEM)
    out = jax.ShapeDtypeStruct((K, 512), F)
    scratch = [
        pltpu.VMEM((NY, 8, EC), F),
        pltpu.VMEM((8, 2, LANES), F),
        pltpu.VMEM((2, OWN, WIN, LANES), F),
        pltpu.VMEM((2, OWN + 1, WIN, LANES), F),
        pltpu.VMEM((OWN + 1, MID, LANES), F),
        pltpu.VMEM((2, OWN + 1, SIDE, LANES), F),
        pltpu.VMEM((2, OWN + 1, SIDE, LANES), F),
        pltpu.VMEM((2 * ROWS * WIN, LANES), BF),
        pltpu.VMEM((2 * ROWS * MID, LANES), BF),
        pltpu.VMEM((2 * (ROWS + 1) * WIN, LANES), F),
        pltpu.VMEM((2 * (ROWS + 1) * MID, LANES), F),
        pltpu.VMEM((2 + 4 * OWN, MID, LANES), F),
        pltpu.VMEM((ITERS, NX, 16, 128), F),
        pltpu.VMEM((ITERS, NZ, 16, 128), F),
        pltpu.VMEM((8, 8, 512), F),
        pltpu.VMEM((8, 8, 512), F),
    ]
    counts = [(NY - 1,), (7,), (5,), (5,), (ITERS, NX - 1), (ITERS, NZ - 1), (7,)]
    scratch += [dma(*count) for count in counts for _ in range(2)]
    return pl.pallas_call(
        kernel,
        out_shape=(out, out),
        in_specs=[vmem, vmem],
        out_specs=(vmem, vmem),
        scratch_shapes=scratch,
        compiler_params=pltpu.CompilerParams(
            collective_id=0, has_side_effects=True, vmem_limit_bytes=56 * 2**20
        ),
        name="resistances",
    )(edges, ground.reshape(2, LANES))


def solution(mesh):
    in_specs = (
        P(("dom", "grp")),
        P(("dom", "grp")),
        P(None, ("dom", "grp")),
        P(("dom", "grp")),
        P(("dom", "grp")),
    )
    out_specs = (P(None, ("dom", "grp")), P(None, ("dom", "grp")))
    return jax.shard_map(
        on_device, mesh=mesh, in_specs=in_specs, out_specs=out_specs, check_vma=False
    )
```

time: 1290 us -> 175 us (0.14)
  blocking collectives: 424 us -> 0 us
  other arithmetic: 415 us -> 1.66 us
  local copies, waits for them, and re-layouts: 215 us -> 5.12 us
  waiting for transfers between devices: 183 us -> 0 us
  Pallas kernels: 0 us -> 167 us
  starting transfers between devices: 34.4 us -> 0 us
  between operations: 14 us -> 0.7 us
    scatter-add x8 -> x0, other arithmetic: 401 us -> none  [edge_scatter(): return acc.at[:, first].add(plus).at[:, tails].add(minus)]
    psum x5 -> x0, blocking collectives: 382 us -> none  [inner(): return lax.psum(partial_value, ('dom', 'grp'))]
    gather x6 -> x0, local copies, waits for them, and re-layouts: 179 us -> none  [on_device(): diff = edge_weights[None, :] * (widened[:, first] - widened[:, tails])]
    pallas_call x0 -> x1, Pallas kernels: none -> 167 us  [on_device(): pl.pallas_call(kernel, out_shape=(out, out), in_specs=[vmem, vmem], out_s...]
    reduce_scatter x4 -> x0, waiting for transfers between devices: 162 us -> none  [fold(): return lax.psum_scatter(middle, 'grp', scatter_dimension=1, tiled=True)]
    all_gather x3 -> x0, blocking collectives: 42.8 us -> none  [on_device(): whole = lax.all_gather(direction, 'grp', axis=1, tiled=True)]
    ppermute x14 -> x0, starting transfers between devices: 34.3 us -> none  [the longest x8 22.7 us: passed_along(): lax.ppermute(value, axis, [(source, source + steps) for source in range(l...]
    ppermute x14 -> x0, waiting for transfers between devices: 20.9 us -> none  [the longest x3 11.4 us: extended(): lax.ppermute(head, axis, [((i + 1) % count, i) for i in range(ends)])]
  transfers between devices with their start and end apart: 18 -> 0, of which waited for: 14 -> 0; matrix products, arithmetic and copies ran while one was open for 1% -> 0% of each run, Pallas kernels for 0% -> 0%
where the time goes in v1:
time: 175 us
  Pallas kernels  167 us (95%)
  local copies, waits for them, and re-layouts  5.12 us (3%)
    pallas_call x1, Pallas kernels, on_device(): pl.pallas_call(kernel, out_shape=(out, out), in_specs=[vmem, vmem], out_s...  167 us
    unnamed x12, local copies, waits for them, and re-layouts  4.26 us

profile of v1, /device:TPU:1, one launch (start us, length us, event | category | flops | bytes accessed | tf_op | source)
XLA Modules:
  0.0 174.6 jit_solution(17615322975583686745)
XLA Ops:
  0.6 0.9 convert_element_type.11
  1.5 0.2 slice_reduce_fusion.1
  1.7 0.0 copy-start.1
  1.7 0.7 copy-done.1
  2.5 0.0 copy-start.2
  2.5 0.7 copy-done.2
  3.2 0.0 copy-start.3
  3.3 0.7 copy-done.3
  4.0 0.1 maximum_bitcast_fusion
  4.1 0.0 copy-start.4
  4.1 0.7 pad_maximum_fusion.edges
  4.8 0.0 copy-done.4
  4.8 0.6 reshape.24.ground
  5.4 167.1 %resistances.1 = (f32[24,512]{1,0:T(8,128)}, f32[24,512]{1,0:T(8,128)}) custom-call(f32[2,8,4096]{2,1,0:T(8,128)} %pad_maximum_fusion.edges, f32[2,256]{1,0:T(2,128)} %reshape.24.ground), custom_call_target="tpu_custom_call" | custom-call | tf_op jit(solution)/shard_map/resistances/pallas_call | solution.py:311
  172.5 0.0 copy-start
  172.6 1.4 copy.9
  174.0 0.0 copy-done
  174.0 0.6 copy.10
  (7 shorter events, 0.1 us)
Async XLA Ops:
  1.7 0.8 copy-start.1
  2.5 0.8 copy-start.2
  3.2 0.8 copy-start.3
  4.1 0.7 copy-start.4
  172.5 1.4 copy-start

commit v2 on v1

v2 whole, which is shorter than its diff:
```python
import functools

import jax
import jax.numpy as jnp
from jax import lax
from jax.experimental import pallas as pl
from jax.experimental.pallas import tpu as pltpu
from jax.sharding import PartitionSpec as P

MESH = pl.DeviceIdType.MESH
BF, F, I = jnp.bfloat16, jnp.float32, jnp.int32
NT = (((1,), (1,)), ((), ()))
K = 24
ITERS = 3
NX, NZ, NY = 4, 8, 4
OWN = 3
ROWS = 2 * OWN
LANES = 256
WIN, MID, SIDE = 32, 16, 8
EC = 4096
WIDE = 1024
COL_H, TILE_H, COL_T, TILE_T, WEIGHT, SIGNS = range(6)


def split(value):
    high = value.astype(BF)
    return high, (value - high.astype(F)).astype(BF)


def onehot(index):
    lanes = lax.broadcasted_iota(I, (LANES, index.shape[1]), 0).astype(F).astype(BF)
    return jnp.where(lanes == index.astype(BF), jnp.ones((), BF), jnp.zeros((), BF))


def edge_row(pre, c, name):
    block, first = c // 2, (c % 2) * (EC // WIDE)
    return jnp.concatenate([pre[block, name, pl.ds(first + q, 1), :] for q in range(EC // WIDE)], axis=1)


def at_tile(row, tiles):
    return lax.broadcasted_iota(I, (tiles, row.shape[1]), 0).astype(F) == row


def spread(mask, parts):
    ones = jnp.where(mask, 1.0, 0.0).astype(BF)
    return jnp.concatenate([ones * parts[k][q] for q in range(2) for k in range(len(parts))], axis=0)


def prepare(eb, pre, block):
    for source, col, tile in ((0, COL_H, TILE_H), (1, COL_T, TILE_T)):
        whole = eb[block, source].astype(I)
        pre[block, col] = (whole & (LANES - 1)).astype(F)
        pre[block, tile] = (whole >> 8).astype(F)
    pre[block, WEIGHT] = eb[block, 2]
    pre[block, SIGNS] = eb[block, 3]


def sketch_tails(pre, c, shift, diffs, total_t):
    weight = edge_row(pre, c, WEIGHT)
    bits = edge_row(pre, c, SIGNS).astype(I) >> shift
    root = jnp.sqrt(weight)
    parts = []
    for k in range(ROWS):
        value = jnp.where(((bits >> k) & 1) == 1, root, -root)
        diffs[c, k : k + 1, :] = value
        parts.append(split(value))
    diffs[c, ROWS : ROWS + 1, :] = weight
    parts.append(split(-weight))
    hot = onehot(edge_row(pre, c, COL_T))
    total_t[...] += lax.dot_general(
        spread(at_tile(edge_row(pre, c, TILE_T), WIN), parts), hot, NT, preferred_element_type=F
    )


def gather_heads(pre, c, tab_h, first_values):
    nh = ROWS * MID
    got = jnp.dot(tab_h[...], onehot(edge_row(pre, c, COL_H)), preferred_element_type=F)
    mask = at_tile(edge_row(pre, c, TILE_H), MID)
    for k in range(ROWS):
        rows = got[MID * k : MID * (k + 1)] + got[nh + MID * k : nh + MID * (k + 1)]
        first_values[c, k] = jnp.where(mask, rows, 0.0).reshape(MID // 8, 8, EC).sum(0)


def apply_tails(pre, c, tab_t, first_values, diffs, energy, total_t):
    nt = ROWS * WIN
    hot = onehot(edge_row(pre, c, COL_T))
    mask = at_tile(edge_row(pre, c, TILE_T), WIN)
    weight = edge_row(pre, c, WEIGHT)
    got = jnp.dot(tab_t[...], hot, preferred_element_type=F)
    parts = []
    for k in range(ROWS):
        rows = got[WIN * k : WIN * (k + 1)] + got[nt + WIN * k : nt + WIN * (k + 1)]
        second = jnp.where(mask, rows, 0.0).reshape(WIN // 8, 8, EC).sum(0)
        gap = jnp.sum(first_values[c, k] - second, axis=0, keepdims=True)
        diff = weight * gap
        diffs[c, k : k + 1, :] = diff
        work = diff * gap
        energy[k : k + 1, :] += sum(work[:, 128 * j : 128 * (j + 1)] for j in range(EC // 128))
        parts.append(split(diff))
    total_t[: 2 * nt] += lax.dot_general(spread(mask, parts), hot, NT, preferred_element_type=F)


def scatter_heads(pre, c, rows, diffs, total_h):
    parts = [split(diffs[c, k : k + 1, :]) for k in range(rows)]
    total_h[: 2 * rows * MID] += lax.dot_general(
        spread(at_tile(edge_row(pre, c, TILE_H), MID), parts),
        onehot(edge_row(pre, c, COL_H)), NT, preferred_element_type=F,
    )


def tables(table, core, tab, first, tiles):
    n, at = ROWS * tiles, OWN * tiles * core
    high, low = split(table[core, :, first : first + tiles])
    tab[at : at + OWN * tiles] = high.reshape(OWN * tiles, LANES)
    tab[n + at : n + at + OWN * tiles] = low.reshape(OWN * tiles, LANES)


def kernel(
    heads, tails, weights, signs, ground, sol, res,
    eb_s, eb, pre, gb, table, acc, in_mid, in_left, in_right, first_values, diffs, energy,
    tab_t, tab_h, total_t, total_h, state, stat_s, stat_x, stat_z, out_s, out_r,
    ag_s, ag_r, gr_s, gr_r, a_s, a_r, b_s, b_r, x_s, x_r, z_s, z_r, o_s, o_r,
):
    dom, grp = lax.axis_index("dom"), lax.axis_index("grp")
    z, x = dom // NX, dom % NX
    y, core = grp // 2, grp % 2
    other = 1 - core
    left, right = (dom + NX * NZ - 1) % (NX * NZ), (dom + 1) % (NX * NZ)
    near = [(dom, 2 * y + other)]
    near += [(left, 2 * y + (core + rc) % 2) for rc in range(2)]
    near += [(right, 2 * y + (core + rc) % 2) for rc in range(2)]
    group = [(dom, (grp + j) % 8) for j in range(1, 8)]
    along_x = [(z * NX + (x + j) % NX, 2 * y + (core + rc) % 2) for j in range(NX) for rc in range(2)]
    along_z = [(((z + j) % NZ) * NX + x, grp) for j in range(1, NZ)]

    barrier = pltpu.get_barrier_semaphore()
    peers = group + near[1:] + along_x[2:] + along_z
    for peer in peers:
        pl.semaphore_signal(barrier, inc=1, device_id=peer, device_id_type=MESH)

    for word in range(2):
        for j in range(8):
            lanes = slice(128 * j, 128 * (j + 1))
            rows = slice(8 * j, 8 * (j + 1))
            eb_s[word, 0, :, lanes] = heads[rows, :].astype(F)
            eb_s[word, 1, :, lanes] = tails[rows, :].astype(F)
            eb_s[word, 2, :, lanes] = weights[rows, :]
        for row in range(8):
            pieces = [signs[word : word + 1, 128 * (8 * j + row) : 128 * (8 * j + row + 1)] for j in range(8)]
            eb_s[word, 3, row : row + 1, :] = jnp.concatenate(pieces, axis=1).astype(F)
    pl.semaphore_wait(barrier, len(peers))

    def send(source, target, sems, at, peer):
        copy = pltpu.make_async_remote_copy(
            src_ref=source, dst_ref=target, send_sem=sems[0].at[at], recv_sem=sems[1].at[at],
            device_id=peer, device_id_type=MESH,
        )
        copy.start()
        return copy

    def finish(copies):
        for copy in copies:
            copy.wait()

    arriving = []
    for j in range(1, NY):
        to = (y + j) % NY
        arriving.append(send(eb_s.at[to // 2], eb.at[y], (ag_s, ag_r), j - 1, (dom, 2 * to + core)))
    grounds = [send(ground, gb.at[grp], (gr_s, gr_r), j - 1, group[j - 1]) for j in range(1, 8)]
    eb[y] = eb_s[y // 2]
    gb[grp] = ground[...]

    def send_borders(rows):
        copies = []
        for rc in range(2):
            theirs = (core + rc) % 2
            copies.append(
                send(acc.at[theirs, :rows, :SIDE], in_right.at[rc, :rows], (b_s, b_r), 1 + rc, near[1 + rc])
            )
            copies.append(
                send(acc.at[theirs, :rows, SIDE + MID :], in_left.at[rc, :rows], (b_s, b_r), 3 + rc, near[3 + rc])
            )
        return copies

    def send_middle(rows):
        return send(acc.at[other, :rows, SIDE : SIDE + MID], in_mid.at[:rows], (b_s, b_r), 0, near[0])

    def folded(k):
        low = in_left[0, k] + in_left[1, k]
        high = in_right[0, k] + in_right[1, k]
        return acc[core, k, SIDE : SIDE + MID] + in_mid[k] + jnp.concatenate([low, high], axis=0)

    def keep_tails(rows):
        n = rows * WIN
        for c in range(2):
            for k in range(OWN + (rows > ROWS)):
                at = WIN * (OWN * c + k if k < OWN else ROWS)
                whole = total_t[at : at + WIN] + total_t[n + at : n + at + WIN]
                acc[c, k] = -whole

    def keep_heads(rows):
        n = rows * MID
        for c in range(2):
            for k in range(OWN + (rows > ROWS)):
                at = MID * (OWN * c + k if k < OWN else ROWS)
                acc[c, k, SIDE : SIDE + MID] += total_h[at : at + MID] + total_h[n + at : n + at + MID]

    def loop(first, last, step):
        def body(c, carry):
            step(c)
            return carry

        lax.fori_loop(first, last, body, 0)

    def lanes_of(value):
        row = jnp.sum(value, axis=0, keepdims=True)
        return row[:, :128] + row[:, 128:]

    DIAG, GROUND, R, PP, S, X = 0, 1, 2, 2 + OWN, 2 + 2 * OWN, 2 + 3 * OWN
    CHUNKS = 2 * NY
    shift = ROWS * (y % 2)

    total_t[...] = jnp.zeros_like(total_t)
    total_h[...] = jnp.zeros_like(total_h)
    for j in range(NY):
        block = (y + NY - j) % NY
        if j:
            arriving[j - 1].wait()
        prepare(eb, pre, block)
        loop(0, 2, lambda half: sketch_tails(pre, 2 * block + half, shift, diffs, total_t))
    keep_tails(ROWS + 1)
    borders = send_borders(OWN + 1)
    loop(0, CHUNKS, lambda c: scatter_heads(pre, c, ROWS + 1, diffs, total_h))
    keep_heads(ROWS + 1)
    middle = send_middle(OWN + 1)
    finish(grounds)
    for j in range(8):
        for row in range(4):
            lanes = slice(128 * (row % 2), 128 * (row % 2 + 1))
            state[GROUND, 2 * j + row // 2 : 2 * j + row // 2 + 1, lanes] = gb[j, row : row + 1, :]
    finish(borders + [middle])
    state[DIAG] = folded(OWN) + state[GROUND]
    for k in range(OWN):
        state[R + k] = folded(k)
        table[core, k, SIDE : SIDE + MID] = state[R + k] / state[DIAG]

    gamma_was = curve_was = None
    for it in range(ITERS):
        mine = table.at[core]
        to_partner = send(mine.at[:, SIDE : SIDE + MID], mine.at[:, SIDE : SIDE + MID], (a_s, a_r), 0, near[0])
        halos = []
        for rc in range(2):
            halos.append(send(mine.at[:, SIDE : 2 * SIDE], mine.at[:, SIDE + MID :], (a_s, a_r), 1 + rc, near[1 + rc]))
            halos.append(send(mine.at[:, MID : SIDE + MID], mine.at[:, :SIDE], (a_s, a_r), 3 + rc, near[3 + rc]))
        total_t[...] = jnp.zeros_like(total_t)
        total_h[...] = jnp.zeros_like(total_h)
        energy[...] = jnp.zeros_like(energy)
        stat_s[it] = jnp.zeros_like(stat_s[it])
        for k in range(OWN):
            u = table[core, k, SIDE : SIDE + MID]
            stat_s[it, core, OWN + k : OWN + k + 1, :] = lanes_of(state[R + k] * u)
            if it:
                stat_s[it, core, 2 * OWN + k : 2 * OWN + k + 1, :] = lanes_of(state[S + k] * u)
        to_partner.wait()
        for c in range(2):
            tables(table, c, tab_h, SIDE, MID)
        loop(0, CHUNKS, lambda c: gather_heads(pre, c, tab_h, first_values))
        finish(halos)
        for c in range(2):
            tables(table, c, tab_t, 0, WIN)
        loop(0, CHUNKS, lambda c: apply_tails(pre, c, tab_t, first_values, diffs, energy, total_t))
        keep_tails(ROWS)
        borders = send_borders(OWN)

        for c in range(2):
            stat_s[it, c, :OWN, :] = energy[OWN * c : OWN * (c + 1), :]
        for k in range(OWN):
            u = table[core, k, SIDE : SIDE + MID]
            stat_s[it, core, k : k + 1, :] += lanes_of(state[GROUND] * u * u)
        slot = 2 * x + core
        copies = []
        for at in range(1, 2 * NX):
            theirs = (core + at % 2) % 2
            copies.append(
                send(stat_s.at[it, theirs], stat_x.at[it, slot], (x_s.at[it], x_r.at[it]), at - 1, along_x[at])
            )
        stat_x[it, slot] = stat_s[it, core]
        loop(0, CHUNKS // 2, lambda c: scatter_heads(pre, c, ROWS, diffs, total_h))
        finish(copies)
        part = stat_x[it, 0]
        for j in range(1, 2 * NX):
            part = part + stat_x[it, j]
        stat_z[it, z] = part
        copies = []
        for j in range(1, NZ):
            here = stat_z.at[it, z]
            copies.append(send(here, here, (z_s.at[it], z_r.at[it]), j - 1, along_z[j - 1]))
        loop(CHUNKS // 2, CHUNKS, lambda c: scatter_heads(pre, c, ROWS, diffs, total_h))
        keep_heads(ROWS)
        middle = send_middle(OWN)
        finish(copies)
        whole = stat_z[it, 0]
        for j in range(1, NZ):
            whole = whole + stat_z[it, j]
        totals = jnp.sum(whole, axis=1, keepdims=True)
        curve, gamma = totals[:OWN], totals[OWN : 2 * OWN]
        if it:
            beta = gamma / gamma_was
            curve = curve + 2.0 * beta * totals[2 * OWN : 3 * OWN] + beta * beta * curve_was
        alpha = gamma / curve
        finish(borders + [middle])
        for k in range(OWN):
            a = alpha[k : k + 1]
            u = table[core, k, SIDE : SIDE + MID]
            image = folded(k) + state[GROUND] * u
            if it:
                b = beta[k : k + 1]
                direction = u + b * state[PP + k]
                along = image + b * state[S + k]
                state[X + k] = state[X + k] + a * direction
            else:
                direction, along = u, image
                state[X + k] = a * direction
            state[PP + k] = direction
            state[S + k] = along
            rest = state[R + k] - a * along
            state[R + k] = rest
            if it < ITERS - 1:
                table[core, k, SIDE : SIDE + MID] = rest / state[DIAG]
        gamma_was, curve_was = gamma, curve

    for g in range(8):
        for k in range(OWN):
            for half in range(2):
                lanes = slice(LANES * half, LANES * (half + 1))
                tile = slice(2 * g + half, 2 * g + half + 1)
                out_s[g, k : k + 1, lanes] = state[X + k, tile, :]
                out_s[g, OWN + k : OWN + k + 1, lanes] = state[R + k, tile, :]
    copies = []
    for j in range(1, 8):
        to = (grp + j) % 8
        copies.append(send(out_s.at[to], out_r.at[grp], (o_s, o_r), j - 1, group[j - 1]))
    out_r[grp] = out_s[grp]
    finish(copies)
    for g in range(8):
        sol[OWN * g : OWN * (g + 1), :] = out_r[g, :OWN, :]
        res[OWN * g : OWN * (g + 1), :] = out_r[g, OWN : 2 * OWN, :]


def on_device(heads, tails, signs, edge_weights, ground):
    dma = lambda *shape: pltpu.SemaphoreType.DMA(shape)
    vmem = pl.BlockSpec(memory_space=pltpu.VMEM)
    out = jax.ShapeDtypeStruct((K, 512), F)
    scratch = [
        pltpu.VMEM((2, 4, 8, WIDE), F),
        pltpu.VMEM((NY, 4, 8, WIDE), F),
        pltpu.VMEM((NY, 6, 8, WIDE), F),
        pltpu.VMEM((8, 4, 128), F),
        pltpu.VMEM((2, OWN, WIN, LANES), F),
        pltpu.VMEM((2, OWN + 1, WIN, LANES), F),
        pltpu.VMEM((OWN + 1, MID, LANES), F),
        pltpu.VMEM((2, OWN + 1, SIDE, LANES), F),
        pltpu.VMEM((2, OWN + 1, SIDE, LANES), F),
        pltpu.VMEM((2 * NY, ROWS, 8, EC), F),
        pltpu.VMEM((2 * NY, 8, EC), F),
        pltpu.VMEM((8, 128), F),
        pltpu.VMEM((2 * ROWS * WIN, LANES), BF),
        pltpu.VMEM((2 * ROWS * MID, LANES), BF),
        pltpu.VMEM((2 * (ROWS + 1) * WIN, LANES), F),
        pltpu.VMEM((2 * (ROWS + 1) * MID, LANES), F),
        pltpu.VMEM((2 + 4 * OWN, MID, LANES), F),
        pltpu.VMEM((ITERS, 2, 16, 128), F),
        pltpu.VMEM((ITERS, 2 * NX, 16, 128), F),
        pltpu.VMEM((ITERS, NZ, 16, 128), F),
        pltpu.VMEM((8, 8, 512), F),
        pltpu.VMEM((8, 8, 512), F),
    ]
    counts = [(NY - 1,), (7,), (5,), (5,), (ITERS, 2 * NX - 1), (ITERS, NZ - 1), (7,)]
    scratch += [dma(*count) for count in counts for _ in range(2)]
    return pl.pallas_call(
        kernel,
        out_shape=(out, out),
        in_specs=[vmem] * 5,
        out_specs=(vmem, vmem),
        scratch_shapes=scratch,
        compiler_params=pltpu.CompilerParams(
            collective_id=0, has_side_effects=True, vmem_limit_bytes=58 * 2**20
        ),
        name="resistances",
    )(
        heads.reshape(64, 128), tails.reshape(64, 128), edge_weights.reshape(64, 128), signs, ground.reshape(4, 128)
    )


def solution(mesh):
    in_specs = (
        P(("dom", "grp")),
        P(("dom", "grp")),
        P(None, ("dom", "grp")),
        P(("dom", "grp")),
        P(("dom", "grp")),
    )
    out_specs = (P(None, ("dom", "grp")), P(None, ("dom", "grp")))
    return jax.shard_map(
        on_device, mesh=mesh, in_specs=in_specs, out_specs=out_specs, check_vma=False
    )
```

time: 175 us -> 136 us (0.78)
  Pallas kernels: 167 us -> 133 us
  local copies, waits for them, and re-layouts: 5.12 us -> 2.06 us
    pallas_call x1, Pallas kernels: 167 us -> 133 us  [on_device(): pl.pallas_call(kernel, out_shape=(out, out), in_specs=[vmem] * 5, out_spe...]
    unnamed x12 -> x4, local copies, waits for them, and re-layouts: 4.26 us -> 2.06 us
where the time goes in v2:
time: 136 us
  Pallas kernels  133 us (98%)
  local copies, waits for them, and re-layouts  2.06 us (2%)
    pallas_call x1, Pallas kernels, on_device(): pl.pallas_call(kernel, out_shape=(out, out), in_specs=[vmem] * 5, out_spe...  133 us

profile of v2, /device:TPU:1, one launch (start us, length us, event | category | flops | bytes accessed | tf_op | source)
XLA Modules:
  0.0 135.9 jit_solution(1217464878086013057)
XLA Ops:
  0.6 133.2 %resistances.1 = (f32[24,512]{1,0:T(8,128)}, f32[24,512]{1,0:T(8,128)}) custom-call(s32[64,128]{1,0:T(8,128)} %bitcast.4, s32[64,128]{1,0:T(8,128)} %bitcast.5, f32[64,128]{1,0:T(8,128)} %bitcast.6, s32[2,8192]{1,0:T(2,128)} %signs.1, f32[4,128]{1,0:T(4,128)} %bitcast.7), custom_call_target="tpu_custom_call" | custom-call | tf_op jit(solution)/shard_map/resistances/pallas_call | solution.py:380
  133.9 0.0 copy-start
  133.9 1.4 %copy.9 = f32[24,512]{1,0:T(8,128)} copy(f32[24,512]{1,0:T(8,128)} %get-tuple-element.4) | data formatting | bytes 98304
  135.3 0.0 copy-done
  135.3 0.6 copy.10
Async XLA Ops:
  133.9 1.4 %copy-start = (f32[24,512]{1,0:T(8,128)S(1)}, f32[24,512]{1,0:T(8,128)}, u32[]{:S(2)}) copy-start(f32[24,512]{1,0:T(8,128)} %get-tuple-element.5) | copy-start | bytes 147460
